TPU v7x, 32 devices: a whole 2x2x4 slice. The times are simulated.
32 devices in a mesh: expert: 8 (over y, x, core), hidden: 4 (over z).
Axes of the slice: x: 2, y: 2, z: 4, core: 2. Of those that a mesh axis runs over, the one named last changes fastest.
Arguments:
- tokens: bfloat16 [16384, 1024], P(('expert', 'hidden')), may hold values from -6 to 6
- token_ids: int32 [16384], P(('expert', 'hidden')), may hold values from 0 to 8007, as said below
- hash_table: int32 [8008], replicated, may hold values from 0 to 15, as said below
- first_gain: float32 [1024], replicated, may hold values from 0.1 to 1.9
- first_bias: float32 [1024], replicated, may hold values from -2 to 2
- project_in: bfloat16 [1024, 3072], replicated, may hold values from -0.1875 to 0.1875
- project_out: bfloat16 [1024, 1024], replicated, may hold values from -2 to 2
- second_gain: float32 [1024], replicated, may hold values from 0.1 to 1.9
- second_bias: float32 [1024], replicated, may hold values from -2 to 2
- expert_in: bfloat16 [16, 1024, 4096], P('expert', None, 'hidden'), may hold values from -0.1875 to 0.1875
- expert_out: bfloat16 [16, 4096, 1024], P('expert', 'hidden'), may hold values from -0.09375 to 0.09375
- cotangent: bfloat16 [16384, 1024], P(('expert', 'hidden')), may hold values from -6 to 6
Outputs:
- block_out: bfloat16 [16384, 1024], P(('expert', 'hidden'))
- grad_tokens: float32 [16384, 1024], P(('expert', 'hidden'))
- grad_first_gain: float32 [1024], replicated
- grad_first_bias: float32 [1024], replicated
- grad_project_in: float32 [1024, 3072], replicated
- grad_project_out: float32 [1024, 1024], replicated
- grad_second_gain: float32 [1024], replicated
- grad_second_bias: float32 [1024], replicated
- grad_expert_in: float32 [16, 1024, 4096], P('expert', None, 'hidden')
- grad_expert_out: float32 [16, 4096, 1024], P('expert', 'hidden')
Inputs may be any that keep to these rules, and one draw needn't show every extreme that they name: Every token id v has hash_table[v] = its expert; each expert is named by 500 ids or one more. `token_ids`: among one device's 512 tokens at most 96 map to one expert through hash_table, and some expert gets exactly 96.
All inputs are finite; a program needn't handle non-finite values.
Results may differ from a plain program's by a relative error of at most 0.013.
Values may be sent and summed in bfloat16 or wider, within the bound.
A program may use at most 256 MiB of HBM per device.

v0:
```python
import functools

import jax
import jax.numpy as jnp
from jax import lax
from jax.experimental import pallas as pl
from jax.experimental.pallas import tpu as pltpu
from jax.sharding import PartitionSpec as P

HEADS = 16
HEAD_DIM = 64
TILE = 256
SPAN = 512
BLOCK = 256
QUAD = 256
EPS = 1e-05
BF = jnp.bfloat16
F32 = jnp.float32


def dot(a, b, dims=((1,), (0,))):
    return lax.dot_general(a, b, (dims, ((), ())), preferred_element_type=F32)


def expert_kernel(local_experts, has, x, cot, eid, w_in, w_out, act_o, dbef_o, part_o, dmem_o):
    tile = pl.program_id(0)
    outs = (act_o, dbef_o, part_o, dmem_o)

    @pl.when(has[tile, 0] == 0)
    def _():
        for out in outs:
            out[...] = jnp.zeros(out.shape, out.dtype)

    for expert in range(local_experts):

        @pl.when(has[tile, expert] > 0)
        def _(expert=expert):
            mine = eid[...] == float(expert)
            before = dot(x[...], w_in[expert])
            d_after = dot(cot[...], w_out[expert], ((1,), (1,)))
            square = before * before
            inner = 0.7978845608028654 * before * (1.0 + 0.044715 * square)
            tanh = jnp.tanh(inner)
            half = 0.5 * (1.0 + tanh)
            act = (before * half).astype(BF)
            slope = half + 0.5 * before * (1.0 - tanh * tanh) * (
                0.7978845608028654 * (1.0 + 0.134145 * square)
            )
            dbef = (d_after * slope).astype(BF)
            part = dot(act, w_out[expert])
            dmem = dot(dbef, w_in[expert], ((1,), (1,)))
            news = (act.astype(F32), dbef.astype(F32), part, dmem)
            for out, new in zip(outs, news):
                old = 0.0 if expert == 0 else out[...].astype(F32)
                out[...] = jnp.where(mine, new, old).astype(BF)


def expert_rows(x, cot, eid, has, w_in, w_out):
    rows, width = x.shape
    experts, _, hidden = w_in.shape
    tiles = rows // TILE
    row_block = pl.BlockSpec((TILE, width), lambda t, has: (t, 0))
    hid_block = pl.BlockSpec((TILE, hidden), lambda t, has: (t, 0))
    whole = lambda shape: pl.BlockSpec(shape, lambda t, has: (0, 0, 0), pipeline_mode=pl.Buffered(1))
    return pl.pallas_call(
        functools.partial(expert_kernel, experts),
        grid_spec=pltpu.PrefetchScalarGridSpec(
            num_scalar_prefetch=1,
            grid=(tiles,),
            in_specs=[
                row_block,
                row_block,
                pl.BlockSpec((TILE, 1), lambda t, has: (t, 0)),
                whole(w_in.shape),
                whole(w_out.shape),
            ],
            out_specs=[hid_block, hid_block, row_block, row_block],
        ),
        out_shape=[
            jax.ShapeDtypeStruct((rows, hidden), BF),
            jax.ShapeDtypeStruct((rows, hidden), BF),
            jax.ShapeDtypeStruct((rows, width), BF),
            jax.ShapeDtypeStruct((rows, width), BF),
        ],
        compiler_params=pltpu.CompilerParams(vmem_limit_bytes=56 * 2**20),
        cost_estimate=pl.CostEstimate(
            flops=8 * rows * width * hidden,
            bytes_accessed=2 * (w_in.size + w_out.size + 6 * rows * width),
            transcendentals=rows * hidden,
        ),
        name="expert_rows",
    )(has, x, cot, eid, w_in, w_out)


def expert_grad_kernel(owner, tile, count, x, cot, eid, act, dbef, g_in, g_out):
    visit = pl.program_id(0)
    expert = owner[visit]

    @pl.when((visit == 0) | (owner[jnp.maximum(visit - 1, 0)] != expert))
    def _():
        g_in[...] = jnp.zeros(g_in.shape, F32)
        g_out[...] = jnp.zeros(g_out.shape, F32)

    @pl.when(visit < count[0])
    def _():
        mine = jnp.where(eid[...] == expert.astype(F32), 1.0, 0.0).astype(BF)
        g_in[0] += dot(x[...], dbef[...] * mine, ((0,), (0,)))
        g_out[0] += dot(act[...] * mine, cot[...], ((0,), (0,)))


def expert_grads(x, cot, eid, has, act, dbef):
    rows, width = x.shape
    hidden = act.shape[1]
    tiles, experts = has.shape
    wanted = has.at[0].set(1).T.reshape(-1)
    order = jnp.cumsum(wanted) - 1
    most = tiles + experts * 4
    count = jnp.sum(wanted).reshape(1)
    visit = jnp.minimum(jnp.arange(most, dtype=jnp.int32), count - 1)
    chosen = (wanted[None, :] > 0) & (order[None, :] == visit[:, None])
    index = jnp.sum(jnp.where(chosen, jnp.arange(tiles * experts, dtype=jnp.int32)[None, :], 0), 1)
    owner, tile = index // tiles, index % tiles
    row_block = pl.BlockSpec((TILE, width), lambda v, owner, tile, count: (tile[v], 0))
    hid_block = pl.BlockSpec((TILE, hidden), lambda v, owner, tile, count: (tile[v], 0))
    return pl.pallas_call(
        expert_grad_kernel,
        grid_spec=pltpu.PrefetchScalarGridSpec(
            num_scalar_prefetch=3,
            grid=(most,),
            in_specs=[
                row_block,
                row_block,
                pl.BlockSpec((TILE, 1), lambda v, owner, tile, count: (tile[v], 0)),
                hid_block,
                hid_block,
            ],
            out_specs=[
                pl.BlockSpec((1, width, hidden), lambda v, owner, tile, count: (owner[v], 0, 0)),
                pl.BlockSpec((1, hidden, width), lambda v, owner, tile, count: (owner[v], 0, 0)),
            ],
        ),
        out_shape=[
            jax.ShapeDtypeStruct((experts, width, hidden), F32),
            jax.ShapeDtypeStruct((experts, hidden, width), F32),
        ],
        compiler_params=pltpu.CompilerParams(vmem_limit_bytes=56 * 2**20),
        cost_estimate=pl.CostEstimate(
            flops=2 * rows * width * hidden,
            bytes_accessed=8 * experts * width * hidden + 6 * rows * width,
            transcendentals=0,
        ),
        name="expert_grads",
    )(owner, tile, count, x, cot, eid, act, dbef)


MESH = pl.DeviceIdType.MESH


def remote(src, dst, send_sem, recv_sem, device):
    return pltpu.make_async_remote_copy(
        src_ref=src,
        dst_ref=dst,
        send_sem=send_sem,
        recv_sem=recv_sem,
        device_id=device,
        device_id_type=MESH,
    )


def position(plane):
    side = lax.div(plane, 2)
    return side, plane + side * (3 - 2 * plane)


def ones_where(mask):
    return jnp.where(mask, 1.0, 0.0).astype(BF)


def halves(pair):
    left = lax.broadcasted_iota(jnp.int32, pair.shape, 1) < HEAD_DIM
    zero = jnp.zeros_like(pair)
    return (jnp.where(left, pair, zero), jnp.where(left, zero, pair))


def join(first, second):
    left = lax.broadcasted_iota(jnp.int32, first.shape, 1) < HEAD_DIM
    return jnp.where(left, first, second)


def tri(block):
    later = lax.broadcasted_iota(jnp.int32, (block, block), 1)
    return later <= lax.broadcasted_iota(jnp.int32, (block, block), 0)


def normalise(values):
    centered = values - jnp.mean(values, -1, keepdims=True)
    spread = jnp.mean(centered * centered, -1, keepdims=True)
    root = lax.rsqrt(spread + EPS)
    return centered * root, root


def attend_kernel(
    tokens, w_q, w_k, w_v, w_o, gain1, bias1, gain2, bias2, place, cot, counts,
    residual, second, q_out, k_out, v_out, att_out, lse, cot_col, all_counts, places,
    normed, known, known_places, col_send, col_recv, near_send, near_recv, far_send, far_recv,
    place_send, place_recv, local_sem,
):
    step = pl.program_id(0)
    rows = tokens.shape[0]
    lanes = 2 * HEAD_DIM
    me, plane = lax.axis_index("expert"), lax.axis_index("hidden")
    planes, devices = known.shape[:2]
    side, r = position(plane)
    middle = r == 1
    step_up = 1 - 2 * side
    up, down = {"hidden": plane + step_up}, {"hidden": plane - step_up}
    other = lambda off: {"expert": lax.rem(me + off, devices)}
    across = lambda off: {"hidden": lax.rem(plane + off, planes)}
    sender = lambda off: lax.rem(me - off + devices, devices)

    def col_copy(way, below):
        piece = cot_col.at[plane]
        return remote(cot, piece, col_send.at[way], col_recv.at[below], down if way else up)

    def place_copy(off, source):
        piece = known_places.at[source]
        return remote(piece, piece, place_send.at[off], place_recv.at[off], across(off))

    def near_copy(off, source):
        piece = known.at[plane, source]
        return remote(piece, piece, near_send.at[off], near_recv.at[off], other(off))

    def far_copy(off, source):
        piece = known.at[source]
        return remote(piece, piece, far_send.at[off], far_recv.at[off], across(off))

    def own_copy():
        return pltpu.make_async_copy(cot, cot_col.at[plane], local_sem)

    def each(act, count):
        def body(off, carry):
            act(off)
            return carry

        lax.fori_loop(1, count, body, 0)

    @pl.when(step == 0)
    def _():
        barrier = pltpu.get_barrier_semaphore()

        def greet(device):
            pl.semaphore_signal(barrier, inc=1, device_id=device, device_id_type=MESH)

        each(lambda off: greet(other(off)), devices)
        each(lambda off: greet(across(off)), planes)
        known[plane, me] = counts[...]
        known_places[plane] = jnp.broadcast_to(place[...], known_places.shape[1:])
        pl.semaphore_wait(barrier, devices + planes - 2)
        each(lambda off: near_copy(off, me).start(), devices)
        each(lambda off: place_copy(off, plane).start(), planes)

        @pl.when(r == 0)
        def _():
            col_copy(0, 0).start()

        @pl.when(middle)
        def _():
            col_copy(0, 1).start()
            col_copy(1, 1).start()

        own_copy().start()

    @pl.when(step == 1)
    def _():
        each(lambda off: near_copy(off, sender(off)).wait_recv(), devices)
        each(lambda off: far_copy(off, plane).start(), planes)

    @pl.when(step == 0)
    def _():
        source = tokens[...].astype(F32)
        normed[...] = (normalise(source)[0] * gain1[...] + bias1[...]).astype(BF)
        residual[...] = source
        lse[...] = jnp.zeros(lse.shape, F32)

    q_out[0] = dot(normed[...], w_q[...]).astype(BF)
    k_out[0] = dot(normed[...], w_k[...]).astype(BF)
    v_out[0] = dot(normed[...], w_v[...]).astype(BF)
    width = q_out.shape[2]
    keep = tri(BLOCK)
    lane = lax.broadcasted_iota(jnp.int32, (BLOCK, lse.shape[1]), 1)
    for pair in range(width // lanes):
        cols = slice(pair * lanes, (pair + 1) * lanes)
        query = q_out[0, :, cols] * jnp.asarray(HEAD_DIM**-0.5, BF)
        keys = halves(k_out[0, :, cols])
        values = v_out[0, :, cols]
        for q_block in range(rows // BLOCK):
            q_rows = slice(q_block * BLOCK, (q_block + 1) * BLOCK)
            results = []
            for head in range(2):
                scores = []
                for k_block in range(q_block + 1):
                    k_rows = slice(k_block * BLOCK, (k_block + 1) * BLOCK)
                    part = dot(query[q_rows], keys[head][k_rows], ((1,), (1,)))
                    scores.append(jnp.where(keep, part, -1e30) if k_block == q_block else part)
                top = functools.reduce(jnp.maximum, [jnp.max(s, -1, keepdims=True) for s in scores])
                weights = [jnp.exp(s - top) for s in scores]
                total = sum(jnp.sum(w, -1, keepdims=True) for w in weights)
                share = 1.0 / total
                out = sum(
                    dot((w * share).astype(BF), values[k * BLOCK : (k + 1) * BLOCK])
                    for k, w in enumerate(weights)
                )
                results.append(out)
                index = step * (width // HEAD_DIM) + 2 * pair + head
                lse[q_rows, :] = jnp.where(lane == index, top + jnp.log(total), lse[q_rows, :])
            att_out[0, q_rows, cols] = join(*results).astype(BF)
    residual[...] += dot(att_out[0], w_o[...])

    @pl.when(step == pl.num_programs(0) - 1)
    def _():
        second[...] = (normalise(residual[...])[0] * gain2[...] + bias2[...]).astype(BF)
        each(lambda off: far_copy(off, lax.rem(plane - off + planes, planes)).wait_recv(), planes)
        each(lambda off: place_copy(off, lax.rem(plane - off + planes, planes)).wait_recv(), planes)
        all_counts[...] = known[...]
        places[...] = known_places[...]
        own_copy().wait()
        col_copy(0, 1).wait_recv()
        col_copy(0, 0).wait_send()

        @pl.when(middle)
        def _():
            col_copy(0, 0).wait_recv()
            col_copy(1, 1).wait_send()

        each(lambda off: place_copy(off, plane).wait_send(), planes)
        each(lambda off: near_copy(off, me).wait_send(), devices)
        each(lambda off: far_copy(off, plane).wait_send(), planes)


def attend(
    devices, planes, tokens, project_in, project_out, gain1, bias1, gain2, bias2, place, cot, counts
):
    rows, width = tokens.shape
    dma = pltpu.SemaphoreType.DMA
    counts = jnp.broadcast_to(jnp.pad(counts, (0, 128 - counts.shape[0]))[None, :], (8, 128))
    known = (planes, devices, 8, 128)
    steps = width // QUAD
    whole = lambda shape: pl.BlockSpec(shape, lambda j: (0, 0))
    third = lambda k: pl.BlockSpec((width, QUAD), lambda j: (0, k * steps + j))
    cols = pl.BlockSpec((1, rows, QUAD), lambda j: (j, 0, 0))
    vector = whole((1, width))
    low = jax.ShapeDtypeStruct((rows, width), BF)
    split = jax.ShapeDtypeStruct((steps, rows, QUAD), BF)
    return pl.pallas_call(
        attend_kernel,
        grid=(steps,),
        in_specs=[whole((rows, width)), third(0), third(1), third(2),
            pl.BlockSpec((QUAD, width), lambda j: (j, 0)), vector, vector, vector, vector,
            whole((1, rows)), whole((rows, width)), whole((8, 128))],
        out_specs=[whole((rows, width)), whole((rows, width)), cols, cols, cols, cols, whole((rows, 128)),
            pl.BlockSpec(memory_space=pl.ANY), pl.BlockSpec(known, lambda j: (0, 0, 0, 0)),
            pl.BlockSpec((planes, 8, rows), lambda j: (0, 0, 0))],
        out_shape=[jax.ShapeDtypeStruct((rows, width), F32), low, split, split, split, split,
            jax.ShapeDtypeStruct((rows, 128), F32), jax.ShapeDtypeStruct((planes, rows, width), BF),
            jax.ShapeDtypeStruct(known, jnp.int32), jax.ShapeDtypeStruct((planes, 8, rows), jnp.int32)],
        scratch_shapes=[pltpu.VMEM((rows, width), BF), pltpu.VMEM(known, jnp.int32),
            pltpu.VMEM((planes, 8, rows), jnp.int32), dma((2,)), dma((2,)), dma((devices,)), dma((devices,)),
            dma((planes,)), dma((planes,)), dma((planes,)), dma((planes,)), dma],
        compiler_params=pltpu.CompilerParams(
            collective_id=0, has_side_effects=True, vmem_limit_bytes=56 * 2**20
        ),
        cost_estimate=pl.CostEstimate(flops=10 * rows * width * width, bytes_accessed=20 * 2**20,
            transcendentals=HEADS * rows * rows),
        name="attend",
    )(tokens, project_in, project_in, project_in, project_out, *(v.reshape(1, width) for v in (gain1, bias1, gain2, bias2)),
        place.reshape(1, rows), cot, counts)


def layer_norm_back(d_normed, xhat, root, gain):
    scaled = d_normed * gain
    d_values = root * (
        scaled
        - jnp.mean(scaled, -1, keepdims=True)
        - xhat * jnp.mean(scaled * xhat, -1, keepdims=True)
    )
    sums = (jnp.sum(d_normed * xhat, 0, keepdims=True), jnp.sum(d_normed, 0, keepdims=True))
    return d_values, sums


def pass_kernel(
    rows, pieces, group,
    x, places, targets, target_rows, cot_col, ends, w_in, w_out,
    x_all, cot_all, act_o, dbef_o, part_o, slope_o, o_down, o_up, own_out, cot_far, cot_slots, d_second,
    slots, arrived, packed_x, packed_c, dense, returned, d_part, from_down, from_up, x_tile, c_tile, stage,
    plane_send, plane_recv, cot_send, cot_recv, far_send, far_recv, back_send, back_recv, ag_send, ag_recv,
    rs_send, rs_down, rs_up, os_send, os_down, os_up, local_sem, stage_sem, own_sem, dense_sem,
):
    me, plane = lax.axis_index("expert"), lax.axis_index("hidden")
    _, devices, chunk, width = slots.shape
    experts = w_in.shape[0]
    height = rows // pieces
    tile_height = group * height
    tiles = pieces // group
    side, r = position(plane)
    middle, end = r == 1, r == 0
    step = 1 - 2 * side
    up, down = {"hidden": plane + step}, {"hidden": plane - step}
    physical = lambda rel: rel + side * (3 - 2 * rel)
    part_of = lambda j: pl.ds(pl.multiple_of(j * height, 16), height)
    tile_of = lambda i: pl.ds(pl.multiple_of(i * tile_height, 16), tile_height)
    peer_of = lambda off: lax.rem(me + off, devices)
    source_of = lambda off: lax.rem(me - off + devices, devices)

    def each(act, first, last):
        def body(i, carry):
            act(i)
            return carry

        lax.fori_loop(first, last, body, 0)

    def forward_rel(p):
        return jnp.where(end | (p > 2), p, jnp.where(p == 0, 1, jnp.where(p == 1, 2, 0)))

    def cot_rel(n):
        at_middle = jnp.where(n == 0, 2, jnp.where(n == 1, 0, jnp.where(n == 2, 3, 1)))
        return jnp.where(end, lax.rem(n + 1, 4), at_middle)

    barrier = pltpu.get_barrier_semaphore()
    greet = lambda device: pl.semaphore_signal(barrier, inc=1, device_id=device, device_id_type=MESH)
    each(lambda off: greet({"expert": peer_of(off)}), 1, devices)
    greet(up)

    @pl.when(middle)
    def _():
        greet(down)

    pl.semaphore_wait(barrier, devices + r)

    def far_copy(index):
        block = physical((0, 2, 3)[index])
        source = (cot_far if index == 2 else cot_col).at[block]
        device = down if index else up
        return remote(source, cot_far.at[block], far_send.at[index], far_recv.at[index], device)

    @pl.when(middle)
    def _():
        far_copy(0).start()
        far_copy(1).start()

    def slots_of(device, block, values):
        row = lax.broadcasted_iota(jnp.int32, (chunk, x.shape[0]), 0) + device * chunk
        return dot(ones_where(row == places[block, 0:1, :]), values[...]).astype(BF)

    def dispatch_copy(off, to, frm):
        return remote(
            slots.at[0, to], arrived.at[frm], plane_send.at[off], plane_recv.at[off], {"expert": to}
        )

    def dispatch(off):
        peer = peer_of(off)
        slots[0, peer] = slots_of(peer, plane, x)
        dispatch_copy(off, peer, me).start()

    each(dispatch, 1, devices)
    arrived[me] = slots_of(me, plane, x)

    def cot_copy(n, off, to, frm):
        slot = lax.rem(n + 1, 2)
        return remote(
            slots.at[slot, to], cot_slots.at[n, frm], cot_send.at[n, off], cot_recv.at[n, off], {"expert": to}
        )

    def cot_own(n):
        return pltpu.make_async_copy(slots.at[lax.rem(n + 1, 2), me], cot_slots.at[n, me], own_sem.at[n])

    def cot_sent(n):
        each(lambda off: cot_copy(n, off, peer_of(off), me).wait_send(), 1, devices)

    def send_cot(n, far):
        block = physical(cot_rel(n))

        def fetch(source):
            one = pltpu.make_async_copy(source.at[block], dense, dense_sem)
            one.start()
            one.wait()

        @pl.when(far)
        def _():
            fetch(cot_far)

        @pl.when(jnp.logical_not(far))
        def _():
            fetch(cot_col)

        def fill(off):
            peer = peer_of(off)
            slots[lax.rem(n + 1, 2), peer] = slots_of(peer, block, dense)
            cot_copy(n, off, peer, me).start()

        each(fill, 1, devices)
        slots[lax.rem(n + 1, 2), me] = slots_of(me, block, dense)
        cot_own(n).start()

    send_cot(jnp.int32(0), jnp.bool_(False))

    def pack(block, j):
        row = lax.broadcasted_iota(jnp.int32, (height, devices * chunk), 0) + j * height
        flat = arrived[...].reshape(devices * chunk, width)
        return dot(ones_where(row == targets[block]), flat).astype(BF)

    def gather_copy(way, block, j, own):
        source = packed_x.at[part_of(j)] if own else x_all.at[block, part_of(j)]
        return remote(
            source, x_all.at[block, part_of(j)], ag_send.at[way, block, j], ag_recv.at[block, j], down if way else up
        )

    @pl.when(middle)
    def _():
        far_copy(0).wait_recv()
        far_copy(2).start()

    each(lambda off: dispatch_copy(off, me, source_of(off)).wait_recv(), 1, devices)

    def send_own(j):
        packed_x[part_of(j)] = pack(plane, j)
        gather_copy(0, plane, j, True).start()

        @pl.when(middle)
        def _():
            gather_copy(1, plane, j, True).start()

    each(send_own, 0, pieces)
    keep_own = pltpu.make_async_copy(packed_x, x_all.at[plane, pl.ds(0, rows)], local_sem.at[0])
    keep_own.start()

    keep_own.wait()

    def got(rel, j):
        gather_copy(0, physical(rel), j, False).wait_recv()

    def relay(rel, way, j):
        got(rel, j)
        gather_copy(way, physical(rel), j, False).start()

    def keep_cot(n):
        there = cot_all.at[physical(cot_rel(n)), pl.ds(0, rows)]
        return pltpu.make_async_copy(packed_c, there, local_sem.at[1])

    def collect_cot(n):
        block = physical(cot_rel(n))

        @pl.when(n > 1)
        def _():
            cot_own(n).wait()

        each(lambda off: cot_copy(n, off, me, source_of(off)).wait_recv(), 1, devices)
        fetch = pltpu.make_async_copy(cot_slots.at[n], arrived, dense_sem)
        fetch.start()

        @pl.when(n > 0)
        def _():
            keep_cot(n).wait()

        fetch.wait()

        def one(j):
            packed_c[part_of(j)] = pack(block, j)

        each(one, 0, pieces)
        keep_cot(n).start()

    def sum_copy(rel, j, buffer, index, sems, device):
        return remote(
            d_part.at[physical(rel), part_of(j)],
            buffer.at[index, part_of(j)],
            rs_send.at[rel, j],
            sems.at[index, j],
            device,
        )

    def add(rel, j, buffer, index, sems):
        sum_copy(rel, j, buffer, index, sems, up).wait_recv()
        block = physical(rel)
        here = d_part[block, part_of(j)].astype(F32)
        d_part[block, part_of(j)] = (here + buffer[index, part_of(j)].astype(F32)).astype(BF)

    def out_copy(rel, j, source, buffer, index, sems, device):
        return remote(
            source, buffer.at[index, part_of(j)], os_send.at[rel, j], sems.at[index, j], device
        )

    def out_send(rel, j):
        source = part_o.at[physical(rel), part_of(j)]
        out_copy(rel, j, source, o_down, rel - 1, os_down, up).start()

    def out_sum(rel, j, buffers):
        pads = [t.at[pl.ds(0, height)] for t in (x_tile, c_tile, stage.at[0])]
        loads = [pltpu.make_async_copy(part_o.at[physical(rel), part_of(j)], pads[0], stage_sem.at[0])]
        loads[0].start()
        for n, (buffer, index, sems) in enumerate(buffers):
            piece = buffer.at[index, part_of(j)]
            out_copy(rel, j, piece, buffer, index, sems, up).wait_recv()
            loads.append(pltpu.make_async_copy(piece, pads[n + 1], stage_sem.at[n + 1]))
            loads[-1].start()
        for load in loads:
            load.wait()
        return sum(t[...].astype(F32) for t in pads[: len(loads)]).astype(BF)

    def out_relay(j):
        held = from_down.at[1, part_of(j)]
        held[...] = out_sum(2, j, [(o_down, 1, os_down)])
        out_copy(2, j, held, o_up, 1, os_up, up).start()

    outs = (act_o, dbef_o, part_o, slope_o)

    def stage_copy(index, block, i):
        return pltpu.make_async_copy(
            stage.at[index], outs[index].at[block, tile_of(i)], stage_sem.at[index]
        )

    def load(array, block, i):
        one = pltpu.make_async_copy(array.at[block, tile_of(i)], x_tile, local_sem.at[0])
        one.start()
        one.wait()

    def chooser(block, i):
        row = lax.broadcasted_iota(jnp.int32, (tile_height, 1), 0) + i * tile_height
        before = [row < ends[block, e : e + 1, 0:1] for e in range(experts)]
        mine = [before[e] & jnp.logical_not(before[e - 1]) if e else before[0] for e in range(experts)]

        def choose(results):
            total = jnp.where(mine[0], results[0], 0.0)
            for mask, result in zip(mine[1:], results[1:]):
                total = jnp.where(mask, result, total)
            return total

        return choose

    def columns(body):
        def one(n, carry):
            body(pl.ds(pl.multiple_of(n * SPAN, SPAN), SPAN))
            return carry

        lax.fori_loop(0, width // SPAN, one, 0)

    def staged(block, i):
        for index in (0, 2, 3):
            stage_copy(index, block, i).wait()

    def forward_tile(block, i):
        load(x_all, block, i)
        choose = chooser(block, i)

        @pl.when(i > 0)
        def _():
            staged(block, i)

        def activate(cols):
            before = choose([dot(x_tile[...], w_in[e, :, cols]) for e in range(experts)])
            square = before * before
            tanh = jnp.tanh(0.7978845608028654 * before * (1.0 + 0.044715 * square))
            half = 0.5 * (1.0 + tanh)
            slope = half + 0.5 * before * (1.0 - tanh * tanh) * (
                0.7978845608028654 * (1.0 + 0.134145 * square)
            )
            stage[0, :, cols] = (before * half).astype(BF)
            stage[3, :, cols] = slope.astype(BF)

        def produce(cols):
            results = [dot(stage[0], w_out[e, :, cols]) for e in range(experts)]
            stage[2, :, cols] = choose(results).astype(BF)

        columns(activate)
        columns(produce)
        for index in (0, 2, 3):
            stage_copy(index, block, i).start()

    def backward_tile(block, i, first):
        load(slope_o, block, i)
        choose = chooser(block, i)

        @pl.when(jnp.logical_not(first))
        def _():
            stage_copy(1, block, i).wait()

        def before_back(cols):
            results = [dot(packed_c[tile_of(i)], w_out[e, cols, :], ((1,), (1,))) for e in range(experts)]
            stage[1, :, cols] = (choose(results) * x_tile[:, cols].astype(F32)).astype(BF)

        def members_back(cols):
            results = [dot(stage[1], w_in[e, cols, :], ((1,), (1,))) for e in range(experts)]
            d_part[block, tile_of(i), cols] = choose(results).astype(BF)

        columns(before_back)
        stage_copy(1, block, i).start()
        columns(members_back)

    def phase(p, carry):
        def come(j):
            @pl.when((p == 1) & middle)
            def _():
                relay(0, 0, j)
                relay(2, 1, j)

            @pl.when((p == 2) & middle)
            def _():
                relay(3, 1, j)

            @pl.when((p > 0) & (p < 4) & end)
            def _():
                got(p, j)

        def ahead(i):
            each(come, i * group, (i + 1) * group)

            @pl.when(p < 4)
            def _():
                forward_tile(physical(forward_rel(p)), i)

            @pl.when((p == 3) & middle)
            def _():
                def pass_on(j):
                    add(2, j, from_down, 1, rs_down)
                    sum_copy(2, j, from_up, 1, rs_up, up).start()

                each(pass_on, i * group, (i + 1) * group)

        each(ahead, 0, tiles)

        @pl.when(p < 4)
        def _():
            staged(plane, 0)

        @pl.when(p < 3)
        def _():
            @pl.when(p == 0)
            def _():
                each(lambda off: dispatch_copy(off, peer_of(off), me).wait_send(), 1, devices)

            @pl.when(p > 0)
            def _():
                cot_sent(p - 1)
                cot_own(p - 1).wait()

            @pl.when((p == 0) & end)
            def _():
                far_copy(1).wait_recv()

            @pl.when((p == 1) & end)
            def _():
                far_copy(2).wait_recv()

            send_cot(p + 1, (p == 1) | ((p == 0) & end))

        @pl.when(p == 4)
        def _():
            @pl.when(end)
            def _():
                each(lambda j: out_send(2, j), 0, pieces)
                each(lambda j: out_send(1, j), 0, pieces)

        rel = cot_rel(p - 1)

        def go(j):
            @pl.when((p < 4) & end)
            def _():
                sum_copy(rel, j, from_down, rel - 1, rs_down, up).start()

            @pl.when((p == 4) & middle)
            def _():
                add(3, j, from_down, 2, rs_down)
                sum_copy(3, j, from_up, 0, rs_up, up).start()

            @pl.when((p == 4) & middle & (j > 0))
            def _():
                add(0, j - 1, from_up, 0, rs_up)
                sum_copy(0, j - 1, from_up, 0, rs_up, down).start()

        def behind(i):
            backward_tile(physical(rel), i, (p == 1) & (i == 0))
            each(go, i * group, (i + 1) * group)

        @pl.when(p > 0)
        def _():
            collect_cot(p - 1)
            each(behind, 0, tiles)

        return carry

    lax.fori_loop(0, 5, phase, 0)
    stage_copy(1, plane, 0).wait()
    keep_cot(jnp.int32(3)).wait()

    @pl.when(middle)
    def _():
        add(0, pieces - 1, from_up, 0, rs_up)
        sum_copy(0, pieces - 1, from_up, 0, rs_up, down).start()

    def last(j):
        @pl.when(middle)
        def _():
            add(1, j, from_down, 0, rs_down)
            add(1, j, from_up, 1, rs_up)

        @pl.when(end)
        def _():
            add(0, j, from_up, 0, rs_up)

    each(last, 0, pieces)

    cot_sent(jnp.int32(2))

    def back_slots(device):
        row = lax.broadcasted_iota(jnp.int32, (rows, chunk), 0)
        return dot(ones_where(row == target_rows[device]), d_part[plane], ((0,), (0,))).astype(BF)

    def back_copy(off, to, frm):
        return remote(
            slots.at[1, to], returned.at[frm], back_send.at[off], back_recv.at[off], {"expert": to}
        )

    def back(off):
        peer = peer_of(off)
        slots[1, peer] = back_slots(peer)
        back_copy(off, peer, me).start()

    each(back, 1, devices)
    returned[me] = back_slots(me)

    @pl.when(middle)
    def _():
        each(out_relay, 0, pieces)

    each(lambda off: back_copy(off, me, source_of(off)).wait_recv(), 1, devices)
    slot = lax.broadcasted_iota(jnp.int32, (devices * chunk, x.shape[0]), 0)
    flat = returned[...].reshape(devices * chunk, width)
    d_second[...] = dot(ones_where(slot == places[plane, 0:1, :]), flat, ((0,), (0,))).astype(BF)

    @pl.when(middle)
    def _():
        def out_last(j):
            d_part[plane, part_of(j)] = out_sum(1, j, [(o_down, 0, os_down), (o_up, 1, os_up)])

        each(out_last, 0, pieces)

    @pl.when(end)
    def _():
        own = pltpu.make_async_copy(part_o.at[plane, pl.ds(0, rows)], d_part.at[plane], local_sem.at[0])
        own.start()
        own.wait()

    own = pltpu.make_async_copy(d_part.at[plane], own_out.at[pl.ds(0, rows)], local_sem.at[1])
    own.start()

    x_tile[...] = jnp.zeros(x_tile.shape, BF)
    whole_tiles = -(-rows // TILE) * TILE
    fills = []
    for array, stop in [(a, whole_tiles) for a in (x_all, cot_all, act_o, dbef_o)] + [(part_o, part_o.shape[1])]:
        for block in range(4):
            for start in range(rows, stop, tile_height):
                fills.append(array.at[block, pl.ds(start, min(tile_height, stop - start))])
    for start in range(rows, own_out.shape[0], tile_height):
        fills.append(own_out.at[pl.ds(start, min(tile_height, own_out.shape[0] - start))])
    for there in fills:
        fill = pltpu.make_async_copy(x_tile.at[pl.ds(0, there.shape[0])], there, local_sem.at[0])
        fill.start()
        fill.wait()
    own.wait()

    each(lambda off: back_copy(off, peer_of(off), me).wait_send(), 1, devices)
    cot_sent(jnp.int32(3))

    @pl.when(middle)
    def _():
        for index in range(3):
            far_copy(index).wait_send()

    def sent(j):
        gather_copy(0, plane, j, True).wait_send()

        @pl.when(middle)
        def _():
            gather_copy(1, plane, j, True).wait_send()
            gather_copy(0, physical(0), j, False).wait_send()
            for rel in (2, 3):
                gather_copy(1, physical(rel), j, False).wait_send()
            for rel in (0, 2, 3):
                sum_copy(rel, j, from_up, 0, rs_up, up).wait_send()
            out_copy(2, j, part_o.at[0, part_of(j)], o_up, 1, os_up, up).wait_send()

        @pl.when(end)
        def _():
            for rel in (1, 2, 3):
                sum_copy(rel, j, from_up, 0, rs_up, up).wait_send()
            for rel in (1, 2):
                out_copy(rel, j, part_o.at[0, part_of(j)], o_up, 1, os_up, up).wait_send()

    each(sent, 0, pieces)


def expert_pass(rows, pieces, group, number, room, x, places, targets, target, cot_col, ends, w_in, w_out):
    devices, _, chunk = target.shape
    width, hidden = w_in.shape[1:]
    planes = cot_col.shape[0]
    height = rows // pieces
    tall = group * height
    here, there = pl.BlockSpec(memory_space=pltpu.VMEM), pl.BlockSpec(memory_space=pl.ANY)
    dma = pltpu.SemaphoreType.DMA
    low = lambda *shape: jax.ShapeDtypeStruct(shape, BF)
    held = lambda *shape: pltpu.VMEM(shape, BF)
    wide = low(planes, devices * chunk, width)
    return pl.pallas_call(
        functools.partial(pass_kernel, rows, pieces, group),
        in_specs=[here] * 4 + [there] + [here] * 3,
        out_specs=[there] * 11 + [here],
        out_shape=[wide] * 4
        + [low(planes, room, width), low(planes, rows, hidden), low(3, rows, width), low(2, rows, width), low(room, width)]
        + [low(*cot_col.shape), low(planes, devices, chunk, width), low(*x.shape)],
        scratch_shapes=[
            held(2, devices, chunk, width),
            held(devices, chunk, width),
            held(rows, width),
            held(rows, width),
            held(*x.shape),
            held(devices, chunk, width),
            held(planes, rows, width),
            held(3, rows, width),
            held(2, rows, width),
            held(tall, width),
            held(height, width),
            held(4, tall, hidden),
            dma((devices,)),
            dma((devices,)),
            dma((planes, devices)),
            dma((planes, devices)),
            dma((3,)),
            dma((3,)),
            dma((devices,)),
            dma((devices,)),
            dma((2, planes, pieces)),
            dma((planes, pieces)),
            dma((planes, pieces)),
            dma((3, pieces)),
            dma((2, pieces)),
            dma((planes, pieces)),
            dma((3, pieces)),
            dma((2, pieces)),
            dma((2,)),
            dma((4,)),
            dma((planes,)),
            dma,
        ],
        compiler_params=pltpu.CompilerParams(
            collective_id=number, has_side_effects=True, vmem_limit_bytes=62 * 2**20
        ),
        cost_estimate=pl.CostEstimate(
            flops=20 * planes * rows * width * hidden,
            bytes_accessed=16 * planes * rows * width,
            transcendentals=planes * rows * hidden,
        ),
        name="expert_pass",
    )(x, places, targets, target, cot_col, ends, w_in, w_out)


def tail_kernel(
    pieces,
    tokens, residual, d_second, cot, q, k, v, att, lse, project_in, project_out, gain1, bias1, gain2,
    target_rows, own_in, partial,
    grad_tokens, summed_grads, small_out, out_slots,
    w_in, w_out, normed, d_branch, d_normed, grads, small, small_plane, small_near, small_far,
    core_buf, half_buf, plane_buf, own, o_far, o_near, mine, slot_tile,
    o_send, o_recv, out_sem, slot_sem,
    ar_send, ar_recv, near_send, near_recv, far_send, far_recv,
    w_sem, local_sem,
):
    me, plane = lax.axis_index("expert"), lax.axis_index("hidden")
    devices, planes = lax.axis_size("expert"), lax.axis_size("hidden")
    width = tokens.shape[1]
    quads, tall, quad = grads.shape
    other = lambda off: {"expert": lax.rem(me + off, devices)}
    across = lambda off: {"hidden": lax.rem(plane + off, planes)}

    barrier = pltpu.get_barrier_semaphore()

    def greet(off, carry):
        pl.semaphore_signal(barrier, inc=1, device_id=other(off), device_id_type=MESH)
        return carry

    lax.fori_loop(1, devices, greet, 0)
    for off in range(1, planes):
        pl.semaphore_signal(barrier, inc=1, device_id=across(off), device_id_type=MESH)

    def weights(j, slot):
        cols = lambda third: pl.ds(pl.multiple_of(third * width + j * quad, quad), quad)
        copies = [
            pltpu.make_async_copy(project_in.at[:, cols(third)], w_in.at[slot, third], w_sem.at[slot, third])
            for third in range(3)
        ]
        rows_out = pl.ds(pl.multiple_of(j * quad, quad), quad)
        copies.append(pltpu.make_async_copy(project_out.at[rows_out], w_out.at[slot], w_sem.at[slot, 3]))
        return copies

    for copy in weights(0, 0):
        copy.start()
    pl.semaphore_wait(barrier, devices - 1 + planes - 1)

    rows = own.shape[0]
    height = rows // pieces
    side = lax.div(plane, 2)
    r = plane + side * (3 - 2 * plane)
    middle = r == 1
    step = 1 - 2 * side
    up, down = {"hidden": plane + step}, {"hidden": plane - step}
    physical = lambda rel: rel + side * (3 - 2 * rel)
    part_of = lambda j: pl.ds(pl.multiple_of(j * height, 16), height)

    def out_copy(kind, j):
        source = partial.at[physical(3), part_of(j)] if kind == 0 else mine.at[kind - 1, part_of(j)]
        there = (o_far if kind == 0 else o_near).at[part_of(j)]
        return remote(source, there, o_send.at[kind, j], o_recv.at[kind, j], down if kind == 2 else up)

    def out_load(index):
        source = own_in if index == 2 else partial.at[physical(3 - 3 * index)]
        return pltpu.make_async_copy(source, own if index == 2 else mine.at[index], out_sem.at[index])

    @pl.when(r == 0)
    def _():
        def body(j, carry):
            out_copy(0, j).start()
            return carry

        lax.fori_loop(0, pieces, body, 0)

    for index in range(3):
        out_load(index).start()

    def out_add(kind, j, target):
        out_copy(kind, j).wait_recv()
        there = o_far if kind == 0 else o_near
        here = target[part_of(j)].astype(F32)
        target[part_of(j)] = (here + there[part_of(j)].astype(F32)).astype(BF)

    def out_turn(j):
        @pl.when(middle & (j < pieces))
        def _():
            out_add(0, j, mine.at[0])
            out_copy(1, j).start()

        @pl.when(middle & (j > 0) & (j <= pieces))
        def _():
            out_add(1, j - 1, mine.at[1])
            out_copy(2, j - 1).start()

        @pl.when((r == 0) & (j > 1) & (j <= pieces + 1))
        def _():
            out_add(2, j - 2, own)

    def out_slot_copy(device):
        slot = lax.rem(device, 2)
        return pltpu.make_async_copy(slot_tile.at[slot], out_slots.at[device], slot_sem.at[slot])

    def out_slot(device, carry):
        @pl.when(device > 1)
        def _():
            out_slot_copy(device - 2).wait()

        row = lax.broadcasted_iota(jnp.int32, (rows, slot_tile.shape[1]), 0)
        mask = ones_where(row == target_rows[device])
        slot_tile[lax.rem(device, 2)] = dot(mask, own[...], ((0,), (0,))).astype(BF)
        out_slot_copy(device).start()
        return carry

    bits = devices.bit_length() - 1
    bit = lambda i: lax.rem(lax.div(me, 1 << i), 2)
    partner = lambda i: {"expert": me + (1 << i) * (1 - 2 * bit(i))}
    half = tall // 2
    part = half // 2
    orders = [list(range(1, bits)), list(range(bits - 1, 0, -1))]
    levels = bits - 1
    last = part >> levels
    slice_len = last // planes

    def segment(a, level):
        start = bit(0) * half + a * part
        for i in range(level):
            start = start + bit(orders[a][i]) * (part >> (i + 1))
        return start

    def span(start, length):
        return pl.ds(pl.multiple_of(start, 16), length)

    slot_of = {}

    def sems(name, c):
        index = slot_of.setdefault(name, len(slot_of))
        return ar_send.at[index, c], ar_recv.at[index, c]

    def core_copy(c):
        source = grads.at[c, span((1 - bit(0)) * half, half)]
        return [remote(source, core_buf.at[c], *sems("core", c), partner(0))]

    def core_end(c):
        keep = span(bit(0) * half, half)
        grads[c, keep] = (grads[c, keep].astype(F32) + core_buf[c].astype(F32)).astype(BF)

    def halve_copy(level, c):
        copies = []
        length = part >> (level + 1)
        for a in range(2):
            i = orders[a][level]
            source = grads.at[c, span(segment(a, level) + (1 - bit(i)) * length, length)]
            buffer = half_buf.at[c, a, pl.ds(part - (part >> level), length)]
            copies.append(remote(source, buffer, *sems(("half", level, a), c), partner(i)))
        return copies

    def halve_end(level, c):
        length = part >> (level + 1)
        for a in range(2):
            keep = span(segment(a, level + 1), length)
            other_half = half_buf[c, a, pl.ds(part - (part >> level), length)]
            grads[c, keep] = (grads[c, keep].astype(F32) + other_half.astype(F32)).astype(BF)

    def plane_span(a, p):
        return span(segment(a, levels) + p * slice_len, slice_len)

    def plane_copy(c):
        copies = []
        for a in range(2):
            for off in range(1, planes):
                source = grads.at[c, plane_span(a, lax.rem(plane + off, planes))]
                buffer = plane_buf.at[c, a, off - 1]
                copies.append(remote(source, buffer, *sems(("plane", a, off), c), across(off)))
        return copies

    def plane_end(c):
        for a in range(2):
            keep = plane_span(a, plane)
            total = grads[c, keep].astype(F32)
            for off in range(planes - 1):
                total = total + plane_buf[c, a, off].astype(F32)
            grads[c, keep] = total.astype(BF)
        copies = [
            pltpu.make_async_copy(
                grads.at[c, plane_span(a, plane)],
                summed_grads.at[c, plane_span(a, plane)],
                local_sem.at[a],
            )
            for a in range(2)
        ]
        for copy in copies:
            copy.start()
        for copy in copies:
            copy.wait()

    def spread_copy(c):
        copies = []
        for a in range(2):
            for off in range(1, planes):
                keep = plane_span(a, plane)
                source, there = grads.at[c, keep], summed_grads.at[c, keep]
                copies.append(remote(source, there, *sems(("spread", a, off), c), across(off)))
        return copies

    def double_copy(level, c):
        copies = []
        for a in range(2):
            have = summed_grads.at[c, span(segment(a, level + 1), part >> (level + 1))]
            names = sems(("double", level, a), c)
            copies.append(remote(have, have, *names, partner(orders[a][level])))
        return copies

    def core_back_copy(c):
        have = summed_grads.at[c, span(bit(0) * half, half)]
        return [remote(have, have, *sems("core_back", c), partner(0))]

    nothing = lambda c: None
    stages = [(core_copy, core_end)]
    for level in range(levels):
        stages.append((functools.partial(halve_copy, level), functools.partial(halve_end, level)))
    stages.append((plane_copy, plane_end))
    stages.append((spread_copy, nothing))
    for level in reversed(range(levels)):
        stages.append((functools.partial(double_copy, level), nothing))
    stages.append((core_back_copy, nothing))

    def finish(stage, c):
        copies, end = stages[stage]
        for copy in copies(c):
            copy.wait_recv()
        for copy in copies(c):
            copy.wait_send()
        end(c)

    def near_copy(off):
        return remote(
            small, small_near.at[off - 1], near_send.at[off - 1], near_recv.at[off - 1], other(off)
        )

    def far_copy(off):
        return remote(
            small_plane, small_far.at[off - 1], far_send.at[off - 1], far_recv.at[off - 1], across(off)
        )

    def each_near(act):
        def body(off, carry):
            act(near_copy(off))
            return carry

        lax.fori_loop(1, devices, body, 0)

    scale = jnp.asarray(HEAD_DIM**-0.5, BF)
    lanes = 2 * HEAD_DIM
    xhat2, root2 = normalise(residual[...])
    d_values, sums = layer_norm_back(d_second[...].astype(F32), xhat2, root2, gain2[...])
    d_residual = cot[...].astype(F32) + d_values
    grad_tokens[...] = d_residual
    d_branch[...] = d_residual.astype(BF)
    small[...] = jnp.zeros(small.shape, F32)
    small[2:3, :], small[3:4, :] = sums
    normed[...] = (normalise(tokens[...].astype(F32))[0] * gain1[...] + bias1[...]).astype(BF)
    d_normed[...] = jnp.zeros(d_normed.shape, F32)

    def quarter(j):
        slot = lax.rem(j, 2)
        for copy in weights(j, slot):
            copy.wait()

        @pl.when(j < quads - 1)
        def _():
            for copy in weights(j + 1, 1 - slot):
                copy.start()

        out = dot(att[j], d_branch[...], ((0,), (0,))).astype(BF)
        for m in range(width // quad):
            grads[j, 3 * width + m * quad : 3 * width + (m + 1) * quad] = out[:, m * quad : (m + 1) * quad]
        d_att = dot(d_branch[...], w_out[slot], ((1,), (1,))).astype(BF)
        d_thirds = attention_back(j, q, k, v, d_att, lse, scale, lanes)
        total = 0.0
        for third, d_third in enumerate(d_thirds):
            grads[j, third * width : (third + 1) * width] = dot(
                normed[...], d_third, ((0,), (0,))
            ).astype(BF)
            total = total + dot(d_third, w_in[slot, third], ((1,), (1,)))
        d_normed[...] += total

        @pl.when(j == quads - 1)
        def _():
            xhat, root = normalise(tokens[...].astype(F32))
            d_first, first_sums = layer_norm_back(d_normed[...], xhat, root, gain1[...])
            grad_tokens[...] += d_first
            small[0:1, :], small[1:2, :] = first_sums

    count = len(stages)

    def tick(t, carry):
        @pl.when(t < quads)
        def _():
            quarter(t)
            for copy in stages[0][0](t):
                copy.start()

        for stage in range(count, 0, -1):
            c = t - stage

            @pl.when((c >= 0) & (c < quads))
            def _(stage=stage, c=c):
                finish(stage - 1, c)
                if stage < count:
                    for copy in stages[stage][0](c):
                        copy.start()

        @pl.when(t == 1)
        def _():
            for index in range(3):
                out_load(index).wait()

        @pl.when((t >= 1) & (t <= 2 + pieces))
        def _():
            out_turn(t - 1)

        @pl.when(t == quads + pieces)
        def _():
            lax.fori_loop(0, devices, out_slot, 0)
            for device in (devices - 2, devices - 1):
                out_slot_copy(device).wait()

        @pl.when(t == quads - 1)
        def _():
            each_near(lambda copy: copy.start())

        @pl.when(t == quads + 1)
        def _():
            each_near(lambda copy: copy.wait_recv())
            each_near(lambda copy: copy.wait_send())
            total = small[...]
            for off in range(devices - 1):
                total = total + small_near[off]
            small_plane[...] = total
            for off in range(1, planes):
                far_copy(off).start()

        @pl.when(t == quads + 3)
        def _():
            for off in range(1, planes):
                far_copy(off).wait_recv()
            for off in range(1, planes):
                far_copy(off).wait_send()
            total = small_plane[...]
            for off in range(planes - 1):
                total = total + small_far[off]
            small_out[...] = total

        return carry

    lax.fori_loop(0, max(quads + count, quads + pieces + 1), tick, 0)

    def outs_sent(j, carry):
        @pl.when(r == 0)
        def _():
            out_copy(0, j).wait_send()

        @pl.when(middle)
        def _():
            out_copy(1, j).wait_send()
            out_copy(2, j).wait_send()

        return carry

    lax.fori_loop(0, pieces, outs_sent, 0)


def attention_back(j, q, k, v, d_att, lse, scale, lanes):
    rows, quad = d_att.shape
    keep = tri(BLOCK)
    blocks = rows // BLOCK
    cut = lambda array, block: array[block * BLOCK : (block + 1) * BLOCK]
    d_q, d_k, d_v = [], [], []
    lane = lax.broadcasted_iota(jnp.int32, (BLOCK, lse.shape[1]), 1)
    for pair in range(quad // lanes):
        cols = slice(pair * lanes, (pair + 1) * lanes)
        query = q[j, :, cols] * scale
        key, value, d_pair = k[j, :, cols], v[j, :, cols], d_att[:, cols]
        keys, values = halves(key), halves(value)
        pair_q, pair_k, pair_v = [], [], []
        for head in range(2):
            index = j * (quad // HEAD_DIM) + 2 * pair + head
            q_parts = []
            k_parts, v_parts = [0.0] * blocks, [0.0] * blocks
            for q_block in range(blocks):
                level = jnp.sum(
                    jnp.where(lane == index, lse[q_block * BLOCK : (q_block + 1) * BLOCK, :], 0.0),
                    -1,
                    keepdims=True,
                )
                shares, d_shares, inner = [], [], 0.0
                for k_block in range(q_block + 1):
                    scores = dot(cut(query, q_block), cut(keys[head], k_block), ((1,), (1,)))
                    share = jnp.exp(scores - level)
                    if k_block == q_block:
                        share = jnp.where(keep, share, 0.0)
                    d_share = dot(cut(d_pair, q_block), cut(values[head], k_block), ((1,), (1,)))
                    inner = inner + jnp.sum(share * d_share, -1, keepdims=True)
                    shares.append(share)
                    d_shares.append(d_share)
                total = 0.0
                for k_block in range(q_block + 1):
                    d_scores = (shares[k_block] * (d_shares[k_block] - inner)).astype(BF)
                    total = total + dot(d_scores, cut(key, k_block))
                    k_parts[k_block] += dot(d_scores, cut(query, q_block), ((0,), (0,)))
                    v_parts[k_block] += dot(
                        shares[k_block].astype(BF), cut(d_pair, q_block), ((0,), (0,))
                    )
                q_parts.append(total * HEAD_DIM**-0.5)
            pair_q.append(jnp.concatenate(q_parts, 0))
            pair_k.append(jnp.concatenate(k_parts, 0))
            pair_v.append(jnp.concatenate(v_parts, 0))
        d_q.append(join(*pair_q).astype(BF))
        d_k.append(join(*pair_k).astype(BF))
        d_v.append(join(*pair_v).astype(BF))
    return [jnp.concatenate(parts, 1) for parts in (d_q, d_k, d_v)]


def tail(
    number, devices, planes, pieces, target, own, partial, tokens, residual, d_second, cot, q, k, v, att, lse, project_in, project_out,
    gain1, bias1, gain2,
):
    tokens_dev, width = tokens.shape
    quads, _, quad = q.shape
    tall = 4 * width
    bits = devices.bit_length() - 1
    part = tall // 4
    slice_len = (part >> (bits - 1)) // planes
    slots = 2 + 4 * (bits - 1) + 4 * (planes - 1)
    chunk = target.shape[2]
    rows = own.shape[0]
    here, there = pl.BlockSpec(memory_space=pltpu.VMEM), pl.BlockSpec(memory_space=pl.ANY)
    dma = pltpu.SemaphoreType.DMA
    low = lambda *shape: pltpu.VMEM(shape, BF)
    full = lambda *shape: pltpu.VMEM(shape, F32)
    return pl.pallas_call(
        functools.partial(tail_kernel, pieces),
        in_specs=[here] * 9 + [there] * 2 + [here] * 4 + [there] * 2,
        out_specs=[here, there, here, there],
        out_shape=[
            jax.ShapeDtypeStruct((tokens_dev, width), F32),
            jax.ShapeDtypeStruct((quads, tall, quad), BF),
            jax.ShapeDtypeStruct((8, width), F32),
            jax.ShapeDtypeStruct((devices, chunk, width), BF),
        ],
        scratch_shapes=[
            low(2, 3, width, quad),
            low(2, quad, width),
            low(tokens_dev, width),
            low(tokens_dev, width),
            full(tokens_dev, width),
            low(quads, tall, quad),
            full(8, width),
            full(8, width),
            full(devices - 1, 8, width),
            full(planes - 1, 8, width),
            low(quads, tall // 2, quad),
            low(quads, 2, part - (part >> (bits - 1)), quad),
            low(quads, 2, planes - 1, slice_len, quad),
            low(rows, width),
            low(rows, width),
            low(rows, width),
            low(2, rows, width),
            low(2, chunk, width),
            dma((3, pieces)),
            dma((3, pieces)),
            dma((3,)),
            dma((2,)),
            dma((slots, quads)),
            dma((slots, quads)),
            dma((devices - 1,)),
            dma((devices - 1,)),
            dma((planes - 1,)),
            dma((planes - 1,)),
            dma((2, 4)),
            dma((2,)),
        ],
        compiler_params=pltpu.CompilerParams(
            collective_id=number, has_side_effects=True, vmem_limit_bytes=62 * 2**20
        ),
        cost_estimate=pl.CostEstimate(
            flops=20 * tokens_dev * width * width,
            bytes_accessed=64 * 2**20,
            transcendentals=HEADS * tokens_dev * tokens_dev,
        ),
        name="tail",
    )(
        tokens, residual, d_second, cot, q, k, v, att, lse, project_in, project_out,
        *(x.reshape(1, width) for x in (gain1, bias1, gain2)), target, own, partial,
    )


def spread_kernel(summed, grad_in, grad_out):
    third = pl.program_id(1)

    @pl.when(third < 3)
    def _():
        grad_in[...] = summed[0].astype(F32)

    @pl.when(third == 3)
    def _():
        quad = summed.shape[2]
        for m in range(grad_out.shape[1] // quad):
            rows = slice(m * quad, (m + 1) * quad)
            grad_out[:, rows] = summed[0, rows].astype(F32)


def spread(summed):
    quads, tall, quad = summed.shape
    width = tall // 4
    return pl.pallas_call(
        spread_kernel,
        grid=(quads, 4),
        in_specs=[pl.BlockSpec((1, width, quad), lambda j, t: (j, t, 0))],
        out_specs=[
            pl.BlockSpec((width, quad), lambda j, t: (0, jnp.minimum(t, 2) * quads + j)),
            pl.BlockSpec((quad, width), lambda j, t: (j, 0)),
        ],
        out_shape=[
            jax.ShapeDtypeStruct((width, 3 * width), F32),
            jax.ShapeDtypeStruct((width, width), F32),
        ],
        compiler_params=pltpu.CompilerParams(vmem_limit_bytes=60 * 2**20),
        name="spread",
    )(summed)


def on_device(
    tokens,
    token_ids,
    hash_table,
    first_gain,
    first_bias,
    project_in,
    project_out,
    second_gain,
    second_bias,
    expert_in,
    expert_out,
    cotangent,
):
    rows_dev, width = tokens.shape
    expert_devs = lax.axis_size("expert")
    hidden_devs = lax.axis_size("hidden")
    local = expert_in.shape[0]
    experts = local * expert_devs
    capacity = 8 * ((3 * rows_dev + 8 * experts - 1) // (8 * experts))
    chunk = local * capacity

    owner = hash_table.at[token_ids].get(mode="promise_in_bounds")
    expert_ids = jnp.arange(experts, dtype=jnp.int32)
    onehot = owner[:, None] == expert_ids[None, :]
    earlier = lax.broadcasted_iota(jnp.int32, (rows_dev, rows_dev), 1) < lax.broadcasted_iota(
        jnp.int32, (rows_dev, rows_dev), 0
    )
    before_count = jnp.dot(earlier.astype(BF), onehot.astype(BF), preferred_element_type=F32)
    counts = jnp.sum(onehot.astype(jnp.int32), 0)
    grouped = counts.reshape(expert_devs, local)
    first_slot = (
        jnp.cumsum(grouped, 1) - grouped + jnp.arange(expert_devs, dtype=jnp.int32)[:, None] * chunk
    ).reshape(experts)
    place = jnp.sum(
        jnp.where(onehot, before_count.astype(jnp.int32) + first_slot[None, :], 0), 1
    )
    residual, second, query, keys, values, attended, lse, cot_col, all_counts, places = attend(
        expert_devs, hidden_devs, tokens, project_in, project_out,
        first_gain, first_bias, second_gain, second_bias, place, cotangent, counts,
    )
    all_counts = all_counts[:, :, 0, :experts].reshape(
        hidden_devs, expert_devs, expert_devs, local
    )
    group = lax.axis_index("expert")
    plane = lax.axis_index("hidden")
    group_counts = lax.dynamic_index_in_dim(all_counts, group, 2, keepdims=False)
    most = jnp.max(jnp.sum(all_counts, (1, 3)))

    starts = jnp.cumsum(group_counts, 2) - group_counts
    totals = jnp.sum(group_counts, 1)
    firsts = jnp.cumsum(totals, 1) - totals
    bases = jnp.cumsum(group_counts, 1) - group_counts + firsts[:, None, :]
    slot = jnp.arange(chunk, dtype=jnp.int32)[None, None, :]
    targets = jnp.full((hidden_devs, expert_devs, chunk), -1, jnp.int32)
    for l in range(local):
        offset = slot - starts[:, :, l : l + 1]
        inside = (offset >= 0) & (offset < group_counts[:, :, l : l + 1])
        targets = jnp.where(inside, bases[:, :, l : l + 1] + offset, targets)
    target_rows = lax.dynamic_index_in_dim(targets, plane, 0, keepdims=False)
    target = target_rows.reshape(-1)

    most_rows = expert_devs * chunk
    ends = jnp.cumsum(totals, 1)
    bounds = jnp.broadcast_to(ends[:, :, None], (hidden_devs, local, 128))
    row = jnp.arange(most_rows, dtype=jnp.int32)[None, :]
    eid = sum((row >= ends[:, l : l + 1]).astype(jnp.int32) for l in range(local))
    has = jnp.stack(
        [jnp.any((eid == l).reshape(-1, TILE), 1).astype(jnp.int32) for l in range(local)], 1
    )
    eid = eid.astype(F32)

    def run(rows, pieces, group, number):
        x_all, cot_all, act, dbef, part, _, _, _, own, _, _, d_second = expert_pass(
            rows, pieces, group, number, room, second, places,
            targets.reshape(hidden_devs, 1, expert_devs * chunk),
            target_rows.reshape(expert_devs, 1, chunk), cot_col,
            bounds, expert_in, expert_out,
        )
        return x_all, cot_all, act, dbef, part, own, d_second, jnp.zeros_like(d_second)

    def run_any():
        send = (place[None, :] == jnp.arange(most_rows, dtype=jnp.int32)[:, None]).astype(BF)
        pack = (target[None, :] == jnp.arange(most_rows, dtype=jnp.int32)[:, None]).astype(BF)

        def gather(values):
            slots = dot(send, values).astype(BF).reshape(expert_devs, chunk, width)
            arrived = lax.all_to_all(slots, "expert", 0, 0, tiled=True)
            packed = dot(pack, arrived.reshape(-1, width)).astype(BF)
            return lax.all_gather(packed, "hidden", axis=0, tiled=True)

        def add_up(partial):
            summed = lax.psum_scatter(partial, "hidden", scatter_dimension=0, tiled=True)
            return dot(pack, summed, ((0,), (0,))).astype(BF).reshape(expert_devs, chunk, width)

        x_rows, cot_rows = gather(second), gather(cotangent)
        act, dbef, part, dmem = expert_rows(
            x_rows, cot_rows, eid.reshape(-1, 1), has, expert_in, expert_out
        )
        returned = lax.all_to_all(add_up(dmem), "expert", 0, 0, tiled=True)
        d_second = dot(send, returned.reshape(-1, width), ((0,), (0,))).astype(BF)
        wide = (hidden_devs, most_rows, width)
        x_rows, cot_rows, act, dbef = (v.reshape(wide) for v in (x_rows, cot_rows, act, dbef))
        returned = lax.all_to_all(add_up(part), "expert", 0, 0, tiled=True)
        produced = dot(send, returned.reshape(-1, width), ((0,), (0,))).astype(BF)
        none = jnp.zeros((hidden_devs, room, width), BF)
        return x_rows, cot_rows, act, dbef, none, none[0], d_second, produced

    plans = [(768, 4, 2, 1), (832, 4, 2, 2), (896, 4, 2, 3)]
    plans = [plan for plan in plans if plan[0] < most_rows and hidden_devs == 4]
    room = max(plan[0] for plan in plans)
    pick = sum((most <= plan[0]).astype(jnp.int32) for plan in plans)
    branches = [run_any] + [functools.partial(run, *plan) for plan in reversed(plans)]
    x_all, cot_all, act, dbef, part, own, d_second, more = lax.switch(pick, branches)

    grad_tokens, summed, small, slots = tail(
        4, expert_devs, hidden_devs, 4, target_rows.reshape(expert_devs, 1, chunk), own, part,
        tokens, residual, d_second, cotangent, query, keys, values,
        attended, lse, project_in, project_out, first_gain, first_bias, second_gain,
    )
    slots, act = lax.optimization_barrier((slots, act))
    returned = lax.all_to_all(slots, "expert", 0, 0, tiled=True)
    slot_of = jnp.arange(most_rows, dtype=jnp.int32)[:, None]
    send = (place[None, :] == slot_of).astype(BF)
    produced = dot(send, returned.reshape(-1, width), ((0,), (0,)))
    block_out = (residual + (produced + more.astype(F32))).astype(BF)
    grad_in, grad_out = spread(summed)
    flat = lambda v: v.reshape(-1, width)
    grad_expert_in, grad_expert_out = expert_grads(
        flat(x_all), flat(cot_all), eid.reshape(-1, 1), has, flat(act), flat(dbef)
    )
    return (
        block_out,
        grad_tokens,
        small[0],
        small[1],
        grad_in,
        grad_out,
        small[2],
        small[3],
        grad_expert_in,
        grad_expert_out,
    )


def solution(mesh):
    rows = P(("expert", "hidden"), None)
    w_in, w_out = P("expert", None, "hidden"), P("expert", "hidden", None)
    return jax.shard_map(
        on_device,
        mesh=mesh,
        in_specs=(
            rows,
            P(("expert", "hidden")),
            P(),
            P(),
            P(),
            P(),
            P(),
            P(),
            P(),
            w_in,
            w_out,
            rows,
        ),
        out_specs=(rows, rows, P(), P(), P(), P(), P(), P(), w_in, w_out),
        check_vma=False,
    )
```

profile of v0, /device:TPU:6, one launch (start us, length us, event | category | flops | bytes accessed | tf_op | source)
XLA Modules:
  0.0 576.6 jit_solution(16234556136005517685)
XLA Ops:
  7.2 0.8 compare_select_fusion
  8.0 3.1 gather_fusion
  11.2 0.1 convert_reduce_fusion
  11.4 0.2 reduce_window_sum.54
  11.5 0.1 reduce_window_sum.55
  11.7 0.1 add.122
  11.8 0.3 fusion.25
  12.0 0.6 broadcast_in_dim.32.counts
  12.6 35.8 %attend.1 = (f32[512,1024]{1,0:T(8,128)}, bf16[512,1024]{1,0:T(8,128)(2,1)}, bf16[4,512,256]{2,1,0:T(8,128)(2,1)}, bf16[4,512,256]{2,1,0:T(8,128)(2,1)}, bf16[4,...) custom-call(bf16[512,1024]{1,0:T(8,128)(2,1)} %tokens.3, ...), custom_call_target="tpu_custom_call" | custom-call | flops 5368709120 | bytes 20971520 | tf_op jit(solution)/shard_map/attend/pallas_call | solution.py:354
  48.5 0.9 fusion.39
  49.5 0.1 fusion.38
  49.7 0.2 reduce_window_sum.58
  49.8 0.2 slice_reduce_fusion.1
  50.0 0.1 copy.45
  50.1 0.4 reduce_window_sum.57
  50.6 0.1 select_select_fusion
  50.7 0.7 fusion.37
  51.4 0.4 fusion.34
  51.7 0.1 copy.46
  51.9 0.1 convert_element_type.136
  51.9 0.1 copy.47
  52.1 0.1 convert_element_type.137
  52.1 0.1 copy.42
  52.3 0.6 reduce_max.9
  54.8 0.6 reshape.353.target_rows
  55.4 0.6 add_convert_fusion.2
  56.0 296.5 %conditional.1 = (bf16[4,1536,1024]{2,1,0:T(8,128)(2,1)}, bf16[4,896,1024]{2,1,0:T(8,128)(2,1)}, bf16[896,1024]{1,0:T(8,128)(2,1)S(1)}, bf16[512,1024]{1,0:T(8,1...) conditional(s32[]{:T(128)} %clamp.3, (s32[8,192]{1,0:T(8,128)S(1)}, ...), branch_computations={%region_12.15_spmd, %region_15.16_spmd, %region_16.17_spmd, %regio... | conditional | flops 77333004288 | bytes 367932128 | solution.py:1605
  64.2 0.7 reshape.331.targets
  64.9 0.6 reshape.332.target_rows
  65.5 0.7 broadcast_in_dim.20.ends
  66.1 284.6 %expert_pass.5 = (bf16[4,1536,1024]{2,1,0:T(8,128)(2,1)}, bf16[4,1536,1024]{2,1,0:T(8,128)(2,1)}, bf16[4,1536,1024]{2,1,0:T(8,128)(2,1)}, bf16[4,1536,1024]{2,1,...) custom-call(bf16[512,1024]{1,0:T(8,128)(2,1)} %get-tuple-element.125, ...), custom_call_target="tpu_custom_call" | custom-call | flops 64424509440 | bytes 50331648 | tf_op jit(solution)/shard_map/cond/branch_3_fun/expert_pass/pallas_call | solution.py:912
  350.8 1.6 broadcast.122
  352.5 147.7 %tail.1 = (f32[512,1024]{1,0:T(8,128)}, bf16[4,4096,256]{2,1,0:T(8,128)(2,1)}, f32[8,1024]{1,0:T(8,128)}, bf16[8,192,1024]{2,1,0:T(8,128)(2,1)}) custom-call(bf16[512,1024]{1,0:T(8,128)(2,1)} %tokens.3, f32[512,1024]{1,0:T(8,128)} %get-tuple-element.178.residual, bf16[512,1024]{1,0:T(8,128)(2,1)} %get-tuple-element.183.d_second, bf16[512,1024]{1,0:T(8,128)(2,1)} %cot.3, ...), custom_call_target="tpu_custom_call" | custom-call | flops 10737418240 | bytes 67108864 | tf_op jit(solution)/shard_map/tail/pallas_call | solution.py:1400
  500.2 5.1 all-to-all-start.4
  505.3 1.3 scatter.4
  506.6 1.3 reduce_sum.67
  507.9 0.8 reshape.368
  508.7 0.7 broadcast_compare_fusion
  509.4 0.1 gt.16
  509.5 2.6 copy.54
  512.1 13.9 %spread.1 = (f32[1024,3072]{1,0:T(8,128)}, f32[1024,1024]{1,0:T(8,128)}) custom-call(bf16[4,4096,256]{2,1,0:T(8,128)(2,1)} %get-tuple-element.197.summed), custom_call_target="tpu_custom_call" | custom-call | tf_op jit(solution)/shard_map/spread/pallas_call | solution.py:1475
  526.7 0.1 add_reduce_fusion
  526.8 0.2 select_reduce_fusion
  527.0 0.6 and_select_fusion
  527.6 0.6 fusion.40
  528.2 34.5 %expert_grads.1 = (f32[2,1024,1024]{2,1,0:T(8,128)}, f32[2,1024,1024]{2,1,0:T(8,128)}) custom-call(s32[32]{0:T(128)} %get-tuple-element.259.owner, s32[32]{0:T(128)} %get-tuple-element.258.tile, s32[1]{0:T(128)} %bitcast.39.count, bf16[6144,1024]{1,0:T(8,128)(2,1)} %get-tuple-element.200.x, bf16[6144,1024]{1,0:T(8,128)(2,1)} %get-tuple-element.201.cot, ...), custom_call_target="tpu_custom_call" | custom-call | flops 12884901888 | bytes 54525952 | tf_op jit(solution)/shard_map/expert_grads/pallas_call | solution.py:125
  562.7 5.2 add_convert_fusion
  567.9 1.3 copy.94
  (38 shorter events, 0.5 us)
Async XLA Ops:
  7.2 0.8 copy-start
  7.2 5.4 copy-start.3
  12.0 44.0 %copy-start.8 = (s32[512]{0:T(512)}, s32[512]{0:T(512)S(1)}, u32[]{:S(2)}) copy-start(s32[512]{0:T(512)S(1)} %fusion.25) | copy-start | bytes 6148
  500.2 9.3 %copy-start.6 = (f32[1,1,4,1536]{3,2,1,0:T(4,128)S(1)}, f32[1,1,4,1536]{3,2,1,0:T(4,128)}, u32[]{:S(2)}) copy-start(f32[1,1,4,1536]{3,2,1,0:T(4,128)} %get-tuple-element.256) | copy-start | bytes 73732
  500.2 62.5 %all-to-all-start.4 = ((bf16[8,192,1024]{2,1,0:T(8,128)(2,1)}), bf16[8,192,1024]{2,1,0:T(8,128)(2,1)S(1)}, u32[]{:S(2)}, u32[]{:S(2)}) async-start(bf16[8,192,1024]{2,1,0:T(8,128)(2,1)} %get-tuple-element.193), calls=%async_computation.6 | async-start | bytes 6291456 | tf_op jit(solution)/shard_map/all_to_all | solution.py:1613
  512.1 15.5 %copy-start.7 = (f32[8,1024]{1,0:T(8,128)S(1)}, f32[8,1024]{1,0:T(8,128)}, u32[]{:S(2)}) copy-start(f32[8,1024]{1,0:T(8,128)} %get-tuple-element.196) | copy-start | bytes 98308
  528.2 34.5 %copy-start.9 = (s32[512]{0:T(512)S(1)}, s32[512]{0:T(512)}, u32[]{:S(2)}) copy-start(s32[512]{0:T(512)} %copy-done.8) | copy-start | bytes 6148
  562.7 5.2 copy-start.2
  562.7 6.5 %copy-start.1 = (s32[8008]{0:T(1024)S(1)}, s32[8008]{0:T(1024)}, u32[]{:S(2)}) copy-start(s32[8008]{0:T(1024)} %param.20) | copy-start | bytes 96100
where the time goes:
time: 588 us; the launch traced here: 577 us
  Pallas kernels  517 us (88%)
  between operations  17.3 us (3%)
  local copies, waits for them, and re-layouts  15.7 us (3%)
  loops' own time  8.35 us (1%)
  other arithmetic  8.11 us (1%)
    pallas_call x1, Pallas kernels, expert_pass(): pl.pallas_call(functools.partial(pass_kernel, rows, pieces, group), in_sp...  285 us
    pallas_call x1, Pallas kernels, tail(): pl.pallas_call(functools.partial(tail_kernel, pieces), in_specs=[here] *...  148 us
    pallas_call x1, Pallas kernels, attend(): pl.pallas_call(attend_kernel, grid=(steps,), in_specs=[whole((rows, width...  35.8 us
    pallas_call x1, Pallas kernels, expert_grads(): pl.pallas_call(expert_grad_kernel, grid_spec=pltpu.PrefetchScalarGridSpec...  34.5 us
    pallas_call x1, Pallas kernels, spread(): pl.pallas_call(spread_kernel, grid=(quads, 4), in_specs=[pl.BlockSpec((1,...  13.9 us
  transfers between devices with their start and end apart: 1, of which 0 were waited for; matrix products, arithmetic and copies ran while one was open for 1% of the time, Pallas kernels for 8%

commit v1 on v0

--- a/solution.py
+++ b/solution.py
@@ -92,7 +92,7 @@
     )(has, x, cot, eid, w_in, w_out)
 
 
-def expert_grad_kernel(owner, tile, count, x, cot, eid, act, dbef, g_in, g_out):
+def expert_grad_kernel(owner, tile, low, high, count, x, cot, act, dbef, g_in, g_out):
     visit = pl.program_id(0)
     expert = owner[visit]
 
@@ -103,40 +103,37 @@
 
     @pl.when(visit < count[0])
     def _():
-        mine = jnp.where(eid[...] == expert.astype(F32), 1.0, 0.0).astype(BF)
+        row = lax.broadcasted_iota(jnp.int32, (TILE, 1), 0)
+        mine = ones_where((row >= low[visit]) & (row < high[visit]))
         g_in[0] += dot(x[...], dbef[...] * mine, ((0,), (0,)))
         g_out[0] += dot(act[...] * mine, cot[...], ((0,), (0,)))
 
 
-def expert_grads(x, cot, eid, has, act, dbef):
+def expert_grads(x, cot, lows, highs, act, dbef):
     rows, width = x.shape
     hidden = act.shape[1]
-    tiles, experts = has.shape
-    wanted = has.at[0].set(1).T.reshape(-1)
+    experts, tiles = lows.shape
+    some = (highs > lows) | (jnp.arange(tiles, dtype=jnp.int32) == 0)[None, :]
+    wanted = some.astype(jnp.int32).reshape(-1)
     order = jnp.cumsum(wanted) - 1
     most = tiles + experts * 4
     count = jnp.sum(wanted).reshape(1)
     visit = jnp.minimum(jnp.arange(most, dtype=jnp.int32), count - 1)
     chosen = (wanted[None, :] > 0) & (order[None, :] == visit[:, None])
-    index = jnp.sum(jnp.where(chosen, jnp.arange(tiles * experts, dtype=jnp.int32)[None, :], 0), 1)
+    choose = lambda values: jnp.sum(jnp.where(chosen, values.reshape(1, -1), 0), 1)
+    index = choose(jnp.arange(tiles * experts, dtype=jnp.int32))
     owner, tile = index // tiles, index % tiles
-    row_block = pl.BlockSpec((TILE, width), lambda v, owner, tile, count: (tile[v], 0))
-    hid_block = pl.BlockSpec((TILE, hidden), lambda v, owner, tile, count: (tile[v], 0))
+    row_block = pl.BlockSpec((TILE, width), lambda v, owner, tile, *_: (tile[v], 0))
+    hid_block = pl.BlockSpec((TILE, hidden), lambda v, owner, tile, *_: (tile[v], 0))
     return pl.pallas_call(
         expert_grad_kernel,
         grid_spec=pltpu.PrefetchScalarGridSpec(
-            num_scalar_prefetch=3,
+            num_scalar_prefetch=5,
             grid=(most,),
-            in_specs=[
-                row_block,
-                row_block,
-                pl.BlockSpec((TILE, 1), lambda v, owner, tile, count: (tile[v], 0)),
-                hid_block,
-                hid_block,
-            ],
+            in_specs=[row_block, row_block, hid_block, hid_block],
             out_specs=[
-                pl.BlockSpec((1, width, hidden), lambda v, owner, tile, count: (owner[v], 0, 0)),
-                pl.BlockSpec((1, hidden, width), lambda v, owner, tile, count: (owner[v], 0, 0)),
+                pl.BlockSpec((1, width, hidden), lambda v, owner, *_: (owner[v], 0, 0)),
+                pl.BlockSpec((1, hidden, width), lambda v, owner, *_: (owner[v], 0, 0)),
             ],
         ),
         out_shape=[
@@ -150,7 +147,7 @@
             transcendentals=0,
         ),
         name="expert_grads",
-    )(owner, tile, count, x, cot, eid, act, dbef)
+    )(owner, tile, choose(lows), choose(highs), count, x, cot, act, dbef)
 
 
 MESH = pl.DeviceIdType.MESH
@@ -1555,11 +1552,9 @@
     ends = jnp.cumsum(totals, 1)
     bounds = jnp.broadcast_to(ends[:, :, None], (hidden_devs, local, 128))
     row = jnp.arange(most_rows, dtype=jnp.int32)[None, :]
-    eid = sum((row >= ends[:, l : l + 1]).astype(jnp.int32) for l in range(local))
-    has = jnp.stack(
-        [jnp.any((eid == l).reshape(-1, TILE), 1).astype(jnp.int32) for l in range(local)], 1
-    )
-    eid = eid.astype(F32)
+    base = jnp.arange(0, most_rows, TILE, dtype=jnp.int32)[None, None, :]
+    in_tile = lambda edge: jnp.clip(edge.T[:, :, None] - base, 0, TILE).reshape(local, -1)
+    lows, highs = in_tile(firsts), in_tile(ends)
 
     def run(rows, pieces, group, number):
         x_all, cot_all, act, dbef, part, _, _, _, own, _, _, d_second = expert_pass(
@@ -1571,6 +1566,11 @@
         return x_all, cot_all, act, dbef, part, own, d_second, jnp.zeros_like(d_second)
 
     def run_any():
+        eid = sum((row >= ends[:, l : l + 1]).astype(jnp.int32) for l in range(local))
+        has = jnp.stack(
+            [jnp.any((eid == l).reshape(-1, TILE), 1).astype(jnp.int32) for l in range(local)], 1
+        )
+        eid = eid.astype(F32)
         send = (place[None, :] == jnp.arange(most_rows, dtype=jnp.int32)[:, None]).astype(BF)
         pack = (target[None, :] == jnp.arange(most_rows, dtype=jnp.int32)[:, None]).astype(BF)
 
@@ -1618,7 +1618,7 @@
     grad_in, grad_out = spread(summed)
     flat = lambda v: v.reshape(-1, width)
     grad_expert_in, grad_expert_out = expert_grads(
-        flat(x_all), flat(cot_all), eid.reshape(-1, 1), has, flat(act), flat(dbef)
+        flat(x_all), flat(cot_all), lows, highs, flat(act), flat(dbef)
     )
     return (
         block_out,

time: 588 us -> 581 us (0.988)
  the two profiles are of different devices: /device:TPU:6 before, /device:TPU:0 now
where the time goes in v1:
time: 581 us; the launch traced here: 570 us
  Pallas kernels  517 us (89%)
  between operations  17.4 us (3%)
  local copies, waits for them, and re-layouts  11.7 us (2%)
  loops' own time  8.38 us (1%)
  other arithmetic  5.82 us (1%)
    pallas_call x1, Pallas kernels, expert_pass(): pl.pallas_call(functools.partial(pass_kernel, rows, pieces, group), in_sp...  285 us
    pallas_call x1, Pallas kernels, tail(): pl.pallas_call(functools.partial(tail_kernel, pieces), in_specs=[here] *...  147 us
    pallas_call x1, Pallas kernels, attend(): pl.pallas_call(attend_kernel, grid=(steps,), in_specs=[whole((rows, width...  38.6 us
    pallas_call x1, Pallas kernels, expert_grads(): pl.pallas_call(expert_grad_kernel, grid_spec=pltpu.PrefetchScalarGridSpec...  32.1 us
    pallas_call x1, Pallas kernels, spread(): pl.pallas_call(spread_kernel, grid=(quads, 4), in_specs=[pl.BlockSpec((1,...  13.9 us
  transfers between devices with their start and end apart: 1, of which 0 were waited for; matrix products, arithmetic and copies ran while one was open for 1% of the time, Pallas kernels for 8%

profile of v1, /device:TPU:0, one launch (start us, length us, event | category | flops | bytes accessed | tf_op | source)
XLA Modules:
  0.0 569.7 jit_solution(5734624556475125576)
XLA Ops:
  7.3 0.1 add.117
  7.4 0.8 compare_select_fusion
  8.2 3.1 gather_fusion
  11.3 0.1 convert_reduce_fusion
  11.5 0.2 reduce_window_sum.54
  11.7 0.1 reduce_window_sum.55
  11.8 0.3 fusion.29
  12.1 0.6 broadcast_in_dim.72.counts
  12.6 38.6 %attend.1 = (f32[512,1024]{1,0:T(8,128)}, bf16[512,1024]{1,0:T(8,128)(2,1)}, bf16[4,512,256]{2,1,0:T(8,128)(2,1)}, bf16[4,512,256]{2,1,0:T(8,128)(2,1)}, bf16[4,...) custom-call(bf16[512,1024]{1,0:T(8,128)(2,1)} %tokens.3, ...), custom_call_target="tpu_custom_call" | custom-call | flops 5368709120 | bytes 20971520 | tf_op jit(solution)/shard_map/attend/pallas_call | solution.py:351
  51.3 0.9 fusion.40
  52.3 0.1 fusion.39
  52.5 0.2 reduce_window_sum.56
  52.6 0.4 reduce_window_sum.58
  53.0 0.1 copy.69
  53.2 0.1 select_select_fusion
  53.3 0.1 copy.66
  53.4 0.6 reduce_max.9
  56.0 0.6 reshape.491.target_rows
  56.6 297.1 %conditional.1 = (bf16[4,1536,1024]{2,1,0:T(8,128)(2,1)}, bf16[4,896,1024]{2,1,0:T(8,128)(2,1)}, bf16[896,1024]{1,0:T(8,128)(2,1)S(1)}, bf16[512,1024]{1,0:T(8,1...) conditional(s32[]{:T(128)} %clamp.49, ...), branch_computations={%region_10.15_spmd, %region_15.16_spmd, %region_16.17_spmd, %regio... | conditional | flops 77333094400 | bytes 368055712 | solution.py:1605
  64.8 0.7 reshape.470.targets
  65.5 0.6 reshape.471.target_rows
  66.1 0.7 broadcast_in_dim.33.ends
  66.8 285.2 %expert_pass.5 = (bf16[4,1536,1024]{2,1,0:T(8,128)(2,1)}, bf16[4,1536,1024]{2,1,0:T(8,128)(2,1)}, bf16[4,1536,1024]{2,1,0:T(8,128)(2,1)}, bf16[4,1536,1024]{2,1,...) custom-call(bf16[512,1024]{1,0:T(8,128)(2,1)} %get-tuple-element.119, ...), custom_call_target="tpu_custom_call" | custom-call | flops 64424509440 | bytes 50331648 | tf_op jit(solution)/shard_map/cond/branch_3_fun/expert_pass/pallas_call | solution.py:909
  352.0 1.6 broadcast.245
  353.8 147.0 %tail.1 = (f32[512,1024]{1,0:T(8,128)}, bf16[4,4096,256]{2,1,0:T(8,128)(2,1)}, f32[8,1024]{1,0:T(8,128)}, bf16[8,192,1024]{2,1,0:T(8,128)(2,1)}) custom-call(bf16[512,1024]{1,0:T(8,128)(2,1)} %tokens.3, f32[512,1024]{1,0:T(8,128)} %get-tuple-element.172.residual, bf16[512,1024]{1,0:T(8,128)(2,1)} %get-tuple-element.177.d_second, bf16[512,1024]{1,0:T(8,128)(2,1)} %cot.3, ...), custom_call_target="tpu_custom_call" | custom-call | flops 10737418240 | bytes 67108864 | tf_op jit(solution)/shard_map/tail/pallas_call | solution.py:1397
  500.8 4.0 all-to-all-start.4
  504.8 0.1 copy.72
  504.9 0.1 copy.71
  505.0 0.1 or.40
  505.2 0.1 sub.224
  505.3 0.1 sub.213
  505.3 0.1 sub.222
  505.5 0.1 sub.221
  505.6 0.1 sub.219
  505.7 0.1 sub.211
  505.8 0.1 or.38
  505.9 0.1 sub.215
  505.9 13.9 %spread.1 = (f32[1024,3072]{1,0:T(8,128)}, f32[1024,1024]{1,0:T(8,128)}) custom-call(bf16[4,4096,256]{2,1,0:T(8,128)(2,1)} %get-tuple-element.191.summed), custom_call_target="tpu_custom_call" | custom-call | tf_op jit(solution)/shard_map/spread/pallas_call | solution.py:1472
  519.9 0.1 sub.233
  520.0 0.1 copy.73
  520.1 0.7 convert_reduce_fusion.1
  521.5 0.1 add_reduce_fusion
  521.7 0.8 select_reduce_fusion
  522.4 0.6 and_select_fusion
  523.0 0.6 fusion.41
  523.6 32.1 %expert_grads.1 = (f32[2,1024,1024]{2,1,0:T(8,128)}, f32[2,1024,1024]{2,1,0:T(8,128)}) custom-call(s32[32]{0:T(128)} %get-tuple-element.277.owner, s32[32]{0:T(128)} %get-tuple-element.276.tile, s32[32]{0:T(128)} %get-tuple-element.258.low, s32[32]{0:T(128)} %get-tuple-element.257.high, s32[1]{0:T(128)} %bitcast.42.count, ...), custom_call_target="tpu_custom_call" | custom-call | flops 12884901888 | bytes 54525952 | tf_op jit(solution)/shard_map/expert_grads/pallas_call | solution.py:128
  555.8 5.2 add_convert_fusion.1
  561.0 1.3 copy.114
  (51 shorter events, 0.7 us)
Async XLA Ops:
  7.2 1.0 copy-start
  7.2 5.5 copy-start.3
  12.0 44.6 %copy-start.9 = (s32[512]{0:T(512)}, s32[512]{0:T(512)S(1)}, u32[]{:S(2)}) copy-start(s32[512]{0:T(512)S(1)} %fusion.29) | copy-start | bytes 6148
  52.4 0.8 copy-start.6
  500.8 4.0 copy-start.7
  500.8 55.0 %all-to-all-start.4 = ((bf16[8,192,1024]{2,1,0:T(8,128)(2,1)}), bf16[8,192,1024]{2,1,0:T(8,128)(2,1)S(1)}, u32[]{:S(2)}, u32[]{:S(2)}) async-start(bf16[8,192,1024]{2,1,0:T(8,128)(2,1)} %get-tuple-element.187), calls=%async_computation.6 | async-start | bytes 6291456 | tf_op jit(solution)/shard_map/all_to_all | solution.py:1613
  505.9 17.1 %copy-start.8 = (f32[8,1024]{1,0:T(8,128)S(1)}, f32[8,1024]{1,0:T(8,128)}, u32[]{:S(2)}) copy-start(f32[8,1024]{1,0:T(8,128)} %get-tuple-element.190) | copy-start | bytes 98308
  523.6 32.1 %copy-start.10 = (s32[512]{0:T(512)S(1)}, s32[512]{0:T(512)}, u32[]{:S(2)}) copy-start(s32[512]{0:T(512)} %copy-done.9) | copy-start | bytes 6148
  555.8 5.2 copy-start.2
  555.8 6.5 %copy-start.1 = (s32[8008]{0:T(1024)S(1)}, s32[8008]{0:T(1024)}, u32[]{:S(2)}) copy-start(s32[8008]{0:T(1024)} %param.18) | copy-start | bytes 96100
